TPU v7x, 32 devices: a whole 2x2x4 slice. The times are simulated.
32 devices in a mesh: groups: 2 (over y), context: 4 (over x, core), tensor: 4 (over z).
Axes of the slice: x: 2, y: 2, z: 4, core: 2. Of those that a mesh axis runs over, the one named last changes fastest.
Arguments:
- tokens: bfloat16 [8192, 1920], P(('groups', 'context'), 'tensor'), parts along dimension 0, may hold values from -6 to 6
- in_weight: bfloat16 [1920, 3, 1920], P(None, None, 'tensor'), may hold values from -0.125 to 0.125
- short_filter: bfloat16 [7, 3, 1920], P(None, None, 'tensor'), may hold values from -2 to 2
- mode_weight: float32 [1920, 16], P('tensor'), may hold values from -1.5 to 1.5
- decay_rate: float32 [1920, 16], P('tensor'), as said below
- out_weight: bfloat16 [1920, 1920], P('tensor'), may hold values from -0.1875 to 0.1875
Outputs:
- mixed: bfloat16 [8192, 1920], P(('groups', 'context'), 'tensor'), parts along dimension 0
There are 2 independent parts, one for each index of `groups`. A program takes and returns all parts, laid end to end along the dimension named above; an argument that names none is the same for every part. Nothing has to cross between parts.
Inputs may be any that keep to these rules, and one draw needn't show every extreme that they name: `decay_rate`: every rate lies between 0.2 / 4096 and 1 / 30.
All inputs are finite; a program needn't handle non-finite values.
Results may differ from a plain program's by a relative error of at most 0.025.
Values may be sent and summed in bfloat16 or wider, within the bound.
A program may use at most 64 MiB of HBM per device.

v0:
```python
import jax
import jax.numpy as jnp
from jax import lax
from jax.sharding import PartitionSpec as P

TAPS = 7


HIGH = lax.Precision.HIGHEST


def shifted(array, axis, by):
    size = lax.axis_size(axis)
    pairs = [(i, i + by) for i in range(size) if 0 <= i + by < size]
    return lax.ppermute(array, axis, pairs)


def block_end(drive, decay):
    tok_rows, channels = drive.shape
    piece_len = min(128, tok_rows)
    count = tok_rows // piece_len
    blocks = drive.reshape(count, piece_len, channels)
    offsets = jnp.arange(piece_len).astype(jnp.float32)
    end_weights = jnp.exp(-decay[None] * (piece_len - offsets)[:, None, None])
    ends = jnp.einsum("bqc,qcn->bcn", blocks, end_weights, precision=HIGH)
    later = (count - 1 - jnp.arange(count)).astype(jnp.float32) * piece_len
    return jnp.sum(jnp.exp(-decay[None] * later[:, None, None]) * ends, 0)


def local_conv(drive, decay, amplitude, state_in):
    tok_rows, channels = drive.shape
    piece_len = min(128, tok_rows)
    count = tok_rows // piece_len
    blocks = drive.reshape(count, piece_len, channels)
    offsets = jnp.arange(piece_len).astype(jnp.float32)
    lag_table = offsets[:, None] - offsets[None, :]
    causal = lag_table >= 0.0
    toeplitz = jnp.zeros((piece_len, piece_len, channels), jnp.float32)
    for mode_number in range(decay.shape[1]):
        toeplitz = toeplitz + amplitude[:, mode_number][None, None, :] * jnp.exp(
            -decay[:, mode_number][None, None, :] * jnp.maximum(lag_table, 0.0)[:, :, None]
        )
    toeplitz = jnp.where(causal[:, :, None], toeplitz, 0.0)
    inside = jnp.einsum("tsc,bsc->btc", toeplitz, blocks, precision=HIGH)
    end_weights = jnp.exp(-decay[None] * (piece_len - offsets)[:, None, None])
    ends = jnp.einsum("bqc,qcn->bcn", blocks, end_weights, precision=HIGH)
    block_ids = jnp.arange(count).astype(jnp.float32)
    distance = block_ids[:, None] - block_ids[None, :] - 1.0
    before = distance >= 0.0
    spread = jnp.where(
        before[:, :, None, None],
        jnp.exp(-decay[None, None] * piece_len * jnp.maximum(distance, 0.0)[:, :, None, None]),
        0.0,
    )
    starts = jnp.einsum("bkcn,kcn->bcn", spread, ends, precision=HIGH)
    starts = starts + jnp.exp(-decay[None] * piece_len * block_ids[:, None, None]) * state_in[None]
    start_weights = amplitude[None] * jnp.exp(-decay[None] * offsets[:, None, None])
    carried = jnp.einsum("qcn,bcn->bqc", start_weights, starts, precision=HIGH)
    return (inside + carried).reshape(tok_rows, channels)


def per_device(tokens, in_weight, short_filter, mode_weight, decay_rate, out_weight):
    tok_rows = tokens.shape[0]
    channels = in_weight.shape[2]
    proj = jnp.einsum(
        "td,dkc->tkc",
        lax.all_gather(tokens, "tensor", axis=1, tiled=True),
        in_weight,
        preferred_element_type=jnp.float32,
    ).astype(jnp.bfloat16)
    rim = shifted(proj[tok_rows - (TAPS - 1) :], "context", 1)
    padded = jnp.concatenate([rim, proj], 0)
    filtered = jnp.zeros((tok_rows, 3, channels), jnp.float32)
    for tap_number in range(TAPS):
        begin = TAPS - 1 - tap_number
        filtered = filtered + short_filter[tap_number].astype(jnp.float32)[None] * padded[
            begin : begin + tok_rows
        ].astype(jnp.float32)
    query = filtered[:, 0]
    drive = filtered[:, 1] * filtered[:, 2]
    amplitude = mode_weight * jnp.sqrt(2.0 * decay_rate)
    zero_state = jnp.zeros(decay_rate.shape, jnp.float32)
    my_start = lax.axis_index("context") * tok_rows
    piece = lax.all_gather(drive.astype(jnp.bfloat16), "context", axis=0, tiled=True).astype(
        jnp.float32
    )
    shard_count = piece.shape[0] // tok_rows

    def one_shard(shard_number, running):
        shard = lax.dynamic_slice_in_dim(piece, shard_number * tok_rows, tok_rows, 0)
        shard_end = (shard_number + 1) * tok_rows
        spacing = (my_start - shard_end).astype(jnp.float32)
        factor = jnp.where(spacing >= 0.0, jnp.exp(-decay_rate * jnp.maximum(spacing, 0.0)), 0.0)
        return running + factor * block_end(shard, decay_rate)

    state_in = lax.fori_loop(0, shard_count, one_shard, zero_state)
    conv = local_conv(drive, decay_rate, amplitude, state_in)
    gated = (query * conv).astype(jnp.bfloat16)
    partial_sums = jnp.dot(gated, out_weight, preferred_element_type=jnp.float32)
    summed = lax.psum_scatter(
        partial_sums.astype(jnp.bfloat16), "tensor", scatter_dimension=1, tiled=True
    )
    return summed


def solution(mesh):
    placed = (
        P(("groups", "context"), "tensor"),
        P(None, None, "tensor"),
        P(None, None, "tensor"),
        P("tensor", None),
        P("tensor", None),
        P("tensor", None),
    )
    return jax.shard_map(
        per_device,
        mesh=mesh,
        in_specs=placed,
        out_specs=P(("groups", "context"), "tensor"),
        check_vma=False,
    )
```

profile of v0, /device:TPU:0, one launch (start us, length us, event | category | flops | bytes accessed | tf_op | source)
XLA Modules:
  0.0 415.1 jit_solution(163364691119471869)
XLA Ops:
  8.4 79.7 %all-gather.4.cloned.1.call-done = bf16[1024,1920]{0,1:T(8,128)(2,1)} async-done(((bf16[1024,480]{0,1:T(8,128)(2,1)}), bf16[1024,1920]{0,1:T(8,128)(2,1)}) %all-gather.4.cloned.1.call-update) | async-done | bytes 3932176 | tf_op jit(solution)/shard_map/all_gather | solution.py:67
  88.1 9.4 %fusion.122 = bf16[1024,3,480]{0,2,1:T(8,128)(2,1)S(1)} fusion(bf16[1920,3,480]{0,2,1:T(8,128)(2,1)} %param.9, bf16[1024,1920]{0,1:T(8,128)(2,1)} %all-gather.4.cloned.1.call-done), kind=kOutput, calls=%fused_computation.137 | convolution fusion | flops 5663784960 | bytes 12410880 | tf_op jit(solution)/shard_map/td,dkc->tkc/dot_general | solution.py:65
  97.7 1.8 collective-permute-start
  100.8 9.6 %multiply_add_fusion = f32[1024,3,480]{0,2,1:T(8,128)S(1)} fusion(bf16[1024,3,480]{0,2,1:T(8,128)(2,1)S(1)} %fusion.122, bf16[6,3,480]{0,2,1:T(8,128)(2,1)S(1)} %collective-permute-done, f32[3,480]{1,0:T(4,128)S(1)} %get-tuple-element.216, f32[3,480]{1,0:T(4,128)S(1)} %get-tuple-element.217, f32[3,480]{1,0:T(4,128)S(1)} %get-tuple-element.218, ...), kind=kLoop, calls=%fused_computation.116 | loop fusion | flops 56033280 | bytes 8904960 | tf_op jit(solution)/shard_map/add | solution.py:76
  110.3 2.6 copy-done.1
  112.9 2.1 fusion.141
  118.1 2.0 copy.42
  121.4 7.9 %fusion.114 = f32[480,16,8]{1,2,0:T(8,128)} fusion(f32[8,128,480]{1,0,2:T(8,128)S(1)} %bitcast.112, f32[128]{0:T(128)S(1)} %broadcast_subtract_fusion, f32[480,16]{1,0:T(8,128)S(1)} %get-tuple-element.262), kind=kOutput, calls=%fused_computation.124 | convolution fusion | flops 95354880 | bytes 2243072 | tf_op jit(solution)/shard_map/bqc,qcn->bcn/dot_general | solution.py:46
  129.3 2.1 copy.39
  132.0 1.9 copy.31
  133.9 18.6 %all-gather.6.cloned.1.call-done = bf16[4096,1,480]{0,2,1:T(8,128)(2,1)} async-done(((bf16[1024,1,480]{0,2,1:T(8,128)(2,1)}), bf16[4096,1,480]{0,2,1:T(8,128)(2,1)}) %all-gather.6.cloned.1.call-update) | async-done | bytes 3932176 | tf_op jit(solution)/shard_map/all_gather | solution.py:84
  152.5 6.2 %bitcast_convert_fusion = f32[4096,480]{0,1:T(8,128)} fusion(bf16[4096,1,480]{0,2,1:T(8,128)(2,1)} %all-gather.6.cloned.1.call-done), kind=kLoop, calls=%fused_computation.117 | loop fusion | flops 1966080 | bytes 11796480 | tf_op jit(solution)/shard_map/convert_element_type | solution.py:84
  158.7 36.5 %while.16 = (s32[]{:T(128)}, f32[480,16]{1,0:T(8,128)S(1)}, s32[]{:T(128)}, f32[480,16]{1,0:T(8,128)S(1)}, f32[1,480,16]{2,1,0:T(8,128)S(1)}, /*index=5*/f32[409...) while((s32[]{:T(128)}, f32[480,16]{1,0:T(8,128)S(1)}, ...), condition=%wide.region_2.3_spmd.clone, body=%wide.region_0.2_spmd.clone.sunk | while | flops 95570208 | bytes 10016043 | solution.py:96
  159.1 1.8 dynamic-slice_bitcast_fusion.2
  161.3 6.6 %fusion.160 = f32[480,16]{1,0:T(8,128)S(1)} fusion(f32[8,128,480]{1,0,2:T(8,128)S(1)} %bitcast.111, f32[128]{0:T(128)S(1)} %convert_subtract_fusion.2, f32[480,16]{1,0:T(8,128)S(1)} %bitcast.114, f32[8]{0:T(128)S(1)} %convert_multiply_fusion.2), kind=kOutput, calls=%fused_computation.4.clone.1 | convolution fusion | flops 95531520 | bytes 2028064 | tf_op jit(solution)/shard_map/while/body/eval_jaxpr/bqc,qcn->bcn/dot_general | solution.py:25
  168.1 1.8 dynamic-slice_bitcast_fusion.2
  170.3 6.6 %fusion.160 = f32[480,16]{1,0:T(8,128)S(1)} fusion(f32[8,128,480]{1,0,2:T(8,128)S(1)} %bitcast.111, f32[128]{0:T(128)S(1)} %convert_subtract_fusion.2, f32[480,16]{1,0:T(8,128)S(1)} %bitcast.114, f32[8]{0:T(128)S(1)} %convert_multiply_fusion.2), kind=kOutput, calls=%fused_computation.4.clone.1 | convolution fusion | flops 95531520 | bytes 2028064 | tf_op jit(solution)/shard_map/while/body/eval_jaxpr/bqc,qcn->bcn/dot_general | solution.py:25
  177.1 1.8 dynamic-slice_bitcast_fusion.2
  179.4 6.6 %fusion.160 = f32[480,16]{1,0:T(8,128)S(1)} fusion(f32[8,128,480]{1,0,2:T(8,128)S(1)} %bitcast.111, f32[128]{0:T(128)S(1)} %convert_subtract_fusion.2, f32[480,16]{1,0:T(8,128)S(1)} %bitcast.114, f32[8]{0:T(128)S(1)} %convert_multiply_fusion.2), kind=kOutput, calls=%fused_computation.4.clone.1 | convolution fusion | flops 95531520 | bytes 2028064 | tf_op jit(solution)/shard_map/while/body/eval_jaxpr/bqc,qcn->bcn/dot_general | solution.py:25
  188.4 6.6 %fusion.160 = f32[480,16]{1,0:T(8,128)S(1)} fusion(f32[8,128,480]{1,0,2:T(8,128)S(1)} %bitcast.111, f32[128]{0:T(128)S(1)} %convert_subtract_fusion.2, f32[480,16]{1,0:T(8,128)S(1)} %bitcast.114, f32[8]{0:T(128)S(1)} %convert_multiply_fusion.2), kind=kOutput, calls=%fused_computation.4.clone.1 | convolution fusion | flops 95531520 | bytes 2028064 | tf_op jit(solution)/shard_map/while/body/eval_jaxpr/bqc,qcn->bcn/dot_general | solution.py:25
  195.2 6.9 %fusion.110 = f32[480,8,128]{2,1,0:T(8,128)S(1)} fusion(f32[480,16,8]{1,2,0:T(8,128)} %copy.31, f32[128]{0:T(128)S(1)} %iota_convert_fusion.1, f32[480,16]{1,0:T(8,128)S(1)} %copy-done.5, f32[480,16]{1,0:T(8,128)S(1)} %get-tuple-element.295, f32[480,16]{1,0:T(8,128)S(1)} %get-tuple-element.138, f32[8]{0:T(128)S(1)} %iota_convert_fusion, ...), kind=kOutput, calls=%fused_computation.120 | convolution fusion | flops 96522240 | bytes 2335264 | tf_op jit(solution)/shard_map/qcn,bcn->bqc/dot_general | solution.py:58
  202.2 127.5 %fusion.134 = f32[480,8,128]{2,1,0:T(8,128)S(1)} fusion(f32[480,8,128]{2,1,0:T(8,128)S(1)} %fusion.110, f32[8,128,480]{1,0,2:T(8,128)S(1)} %bitcast.113, f32[480]{0:T(512)S(1)} %bitcast.147, f32[480]{0:T(512)S(1)} %bitcast.117, f32[480]{0:T(512)S(1)} %bitcast.133, f32[480]{0:T(512)S(1)} %bitcast.118, f32[480]{0:T(512)S(1)} %bitcast.134, ...), kind=kOutput, calls=%fused_computation.152 | convolution fusion | flops 1132953600 | bytes 6041600 | tf_op jit(solution)/shard_map/tsc,bsc->btc/dot_general | solution.py:44
  329.8 5.7 %convolution_convert_fusion = bf16[1024,1920]{0,1:T(8,128)(2,1)} fusion(bf16[480,1920]{1,0:T(8,128)(2,1)S(1)} %copy-done, f32[60,8,8,128]{3,2,1,0:T(8,128)S(1)} %bitcast.148, f32[1024,3,480]{0,2,1:T(8,128)} %copy-done.1), kind=kOutput, calls=%fused_computation.127 | convolution fusion | flops 1890385920 | bytes 9707520 | tf_op jit(solution)/shard_map/dot_general | solution.py:99
  335.5 72.8 %reduce-scatter.2.cloned.1.call-done = bf16[1024,480]{0,1:T(8,128)(2,1)} async-done(((bf16[1024,1920]{0,1:T(8,128)(2,1)}), bf16[1024,480]{0,1:T(8,128)(2,1)}) %reduce-scatter.2.cloned.1.call-update) | async-done | bytes 983056 | tf_op jit(solution)/shard_map/reduce_scatter | solution.py:100
  (69 shorter events, 12.2 us)
Async XLA Ops:
  6.5 323.2 %copy-start = (bf16[480,1920]{1,0:T(8,128)(2,1)S(1)}, bf16[480,1920]{1,0:T(8,128)(2,1)}, u32[]{:S(2)}) copy-start(bf16[480,1920]{1,0:T(8,128)(2,1)} %param.13) | copy-start | bytes 5529604
  6.5 81.6 %all-gather.4.cloned.1.call-start = ((), (), s32[]{:S(2)}) async-start(), calls=%async_computation.1 | async-start | bytes 4915200 | tf_op jit(solution)/shard_map/all_gather | solution.py:67
  7.3 145.2 %all-gather.6.cloned.1.call-start = ((), (), s32[]{:S(2)}) async-start(), calls=%async_computation.3 | async-start | bytes 4915200 | tf_op jit(solution)/shard_map/all_gather | solution.py:84
  97.7 3.1 collective-permute-start
  110.3 2.6 copy-start.1
  112.9 2.3 copy-start.4
  112.9 3.3 copy-start.7
  115.0 293.4 %reduce-scatter.2.cloned.1.call-start = ((), (), s32[]{:S(2)}) async-start(), calls=%async_computation.2 | async-start | bytes 4915200 | tf_op jit(solution)/shard_map/reduce_scatter | solution.py:100
  120.1 1.3 copy-start.2
  133.9 24.8 %copy-start.6 = (f32[1,480,16]{2,1,0:T(8,128)S(1)}, f32[1,480,16]{2,1,0:T(8,128)}, u32[]{:S(2)}) copy-start(f32[1,480,16]{2,1,0:T(8,128)} %get-tuple-element.263) | copy-start | bytes 92164
  158.7 36.6 %copy-start.5 = (f32[480,16]{1,0:T(8,128)S(1)}, f32[480,16]{1,0:T(8,128)}, u32[]{:S(2)}) copy-start(f32[480,16]{1,0:T(8,128)} %copy.23) | copy-start | bytes 92164
  195.2 7.0 %copy-start.3 = (f32[60,8,8,128]{3,2,1,0:T(8,128)S(1)}, f32[60,8,8,128]{3,2,1,0:T(8,128)}, u32[]{:S(2)}) copy-start(f32[60,8,8,128]{3,2,1,0:T(8,128)} %copy-done.2) | copy-start | bytes 5898244
  195.2 7.0 %copy-start.8 = (f32[480,1]{0,1:T(1,128)S(1)}, f32[480,1]{0,1:T(1,128)}, u32[]{:S(2)}) copy-start(f32[480,1]{0,1:T(1,128)} %get-tuple-element.205) | copy-start | bytes 5764
  195.2 7.0 %copy-start.9 = (f32[480,1]{0,1:T(1,128)S(1)}, f32[480,1]{0,1:T(1,128)}, u32[]{:S(2)}) copy-start(f32[480,1]{0,1:T(1,128)} %get-tuple-element.206) | copy-start | bytes 5764
  195.2 7.0 %copy-start.10 = (f32[480,1]{0,1:T(1,128)S(1)}, f32[480,1]{0,1:T(1,128)}, u32[]{:S(2)}) copy-start(f32[480,1]{0,1:T(1,128)} %get-tuple-element.207) | copy-start | bytes 5764
  195.2 7.0 %copy-start.11 = (f32[480,1]{0,1:T(1,128)S(1)}, f32[480,1]{0,1:T(1,128)}, u32[]{:S(2)}) copy-start(f32[480,1]{0,1:T(1,128)} %get-tuple-element.208) | copy-start | bytes 5764
Sparse Core Ops, SparseCore 0:
  8.9 79.1 all-gather.3
  115.1 37.3 all-gather.5
  335.6 72.6 reduce-scatter.1
where the time goes:
time: 420 us; the launch traced here: 415 us
  matrix products  184 us (44%)
  waiting for transfers between devices  173 us (41%)
  other arithmetic  21.6 us (5%)
  local copies, waits for them, and re-layouts  20 us (5%)
  between operations  13.5 us (3%)
    dot_general x1, matrix products, local_conv(): inside = jnp.einsum('tsc,bsc->btc', toeplitz, blocks, precision=HIGH)  128 us
    all_gather x1, waiting for transfers between devices, per_device(): lax.all_gather(tokens, 'tensor', axis=1, tiled=True)  79.7 us
    reduce_scatter x1, waiting for transfers between devices, per_device(): lax.psum_scatter(partial_sums.astype(jnp.bfloat16), 'tensor', scatter_dim...  72.8 us
    dot_general x4, matrix products, block_end(): ends = jnp.einsum('bqc,qcn->bcn', blocks, end_weights, precision=HIGH)  26.5 us
    all_gather x1, waiting for transfers between devices, per_device(): lax.all_gather(drive.astype(jnp.bfloat16), 'context', axis=0, tiled=True)  18.6 us
    add x1, other arithmetic, per_device(): filtered + short_filter[tap_number].astype(jnp.float32)[None] * padded[be...  9.55 us
    dot_general x1, matrix products, per_device(): jnp.einsum('td,dkc->tkc', lax.all_gather(tokens, 'tensor', axis=1, tiled=...  9.42 us
    while x8, local copies, waits for them, and re-layouts  8.8 us
  transfers between devices with their start and end apart: 4, of which 4 were waited for; matrix products, arithmetic and copies ran while one was open for 4% of the time, Pallas kernels for 0%

commit v1 on v0

v1 whole, which is shorter than its diff:
```python
import functools

import jax
import jax.numpy as jnp
from jax import lax
from jax.experimental import pallas as pl
from jax.experimental.pallas import tpu as pltpu
from jax.sharding import PartitionSpec as P

TAPS = 7
HEAD = 8
RIM = 16
MESH = pl.DeviceIdType.MESH


def kernel(
    n, contexts, count, tok, win_hbm, wout_hbm, filt, decay, amp, decay_block, out,
    gathered, rim, win, wout, window, query, drive, gated, state, ends, part, landed,
    local_sem, rim_send, rim_recv, ag_send, ag_recv, end_send, end_recv, rs_send, rs_recv,
):
    rows, ch = tok.shape
    piece = rows // count
    z = lax.axis_index("tensor")
    k = lax.axis_index("context")

    loads = [
        pltpu.make_async_copy(tok, gathered.at[z], local_sem.at[0]),
        pltpu.make_async_copy(win_hbm, win, local_sem.at[1]),
        pltpu.make_async_copy(wout_hbm, wout, local_sem.at[2]),
    ]
    for load in loads:
        load.start()

    barrier = pltpu.get_barrier_semaphore()

    def signal(here, context, tensor):
        @pl.when(here)
        def _():
            pl.semaphore_signal(
                barrier, inc=1, device_id={"context": context, "tensor": tensor}, device_id_type=MESH
            )

    peers = [(z > 0, k, z - 1), (z < n - 1, k, z + 1)]
    for j in range(contexts):
        peers.append((k != j, j, z))
    for step in (-1, 1):
        for zz in range(n):
            peers.append(((k + step >= 0) & (k + step < contexts) & (z != zz), k + step, zz))
    for here, context, tensor in peers:
        signal(here, context, tensor)
    total = functools.reduce(lambda x, y: x + y, [here.astype(jnp.int32) for here, _, _ in peers])
    pl.semaphore_wait(barrier, total)

    def block(c):
        return pl.ds(pl.multiple_of(c * piece, piece), piece)

    def gather_copy(way, src, origin, c):
        side = 0 if way > 0 else 1
        return pltpu.make_async_remote_copy(
            src_ref=src,
            dst_ref=gathered.at[origin, block(c)],
            send_sem=ag_send.at[side, origin, c],
            recv_sem=ag_recv.at[origin, c],
            device_id={"tensor": z + way},
            device_id_type=MESH,
        )

    def send_own(c):
        for way, here in ((1, z < n - 1), (-1, z > 0)):
            @pl.when(here)
            def _():
                gather_copy(way, tok.at[block(c)], z, c).start()

    def rim_copy(slot, zz):
        return pltpu.make_async_remote_copy(
            src_ref=tok.at[pl.ds(rows - RIM, RIM)],
            dst_ref=rim.at[slot],
            send_sem=rim_send.at[zz],
            recv_sem=rim_recv.at[slot],
            device_id={"context": k + 1, "tensor": zz},
            device_id_type=MESH,
        )

    @pl.when(k < contexts - 1)
    def _():
        for zz in range(n):
            rim_copy(z, zz).start()

    send_own(0)
    for load in loads:
        load.wait()
    state[...] = jnp.zeros_like(state)

    def project(stream, load):
        acc = jnp.dot(load(0), win[stream, 0], preferred_element_type=jnp.float32)
        for o in range(1, n):
            acc += jnp.dot(load(o), win[stream, o], preferred_element_type=jnp.float32)
        return acc.astype(jnp.bfloat16).astype(jnp.float32)

    def first_half(c):
        @pl.when((c == 0) & (k == 0))
        def _():
            for stream in range(3):
                window[stream, pl.ds(0, HEAD)] = jnp.zeros((HEAD, ch), jnp.float32)

        @pl.when((c == 0) & (k > 0))
        def _():
            for o in range(n):
                rim_copy(o, 0).wait_recv()
            for stream in range(3):
                window[stream, pl.ds(0, HEAD)] = project(stream, lambda o: rim[o])[RIM - HEAD :]

        for stream in range(3):
            window[stream, pl.ds(HEAD, piece)] = project(stream, lambda o: gathered[o, block(c)])

        def filter_step(r, carry):
            streams = []
            for stream in range(3):
                seen = window[stream, pl.ds(pl.multiple_of(r * 16, 8), 16 + HEAD)]
                total = filt[stream, pl.ds(0, 1)] * seen[HEAD:]
                for tap in range(1, TAPS):
                    total += filt[stream, pl.ds(tap, 1)] * seen[HEAD - tap : HEAD - tap + 16]
                streams.append(total)
            at = pl.ds(pl.multiple_of(c * piece + r * 16, 16), 16)
            query[at] = streams[0]
            drive[at] = streams[1] * streams[2]
            return carry

        lax.fori_loop(0, piece // 16, filter_step, 0)
        for stream in range(3):
            window[stream, pl.ds(0, HEAD)] = window[stream, pl.ds(piece, HEAD)]

        factor = decay[...]

        def state_step(r, now):
            u = drive[pl.ds(pl.multiple_of(c * piece + r * 8, 8), 8)]
            for t in range(8):
                now = now * factor + u[t : t + 1]
            return now

        state[...] = lax.fori_loop(0, piece // 8, state_step, state[...])

    def gather_step(i, carry):
        @pl.when(i + 1 < count)
        def _():
            send_own(i + 1)

        for d in range(n - 1, 0, -1):
            c = i - d
            for way, origin, more in ((1, z - d, z < n - 1), (-1, z + d, z > 0)):
                @pl.when((c >= 0) & (c < count) & (origin >= 0) & (origin < n))
                def _():
                    gather_copy(way, gathered.at[origin, block(c)], origin, c).wait_recv()

                    @pl.when(more)
                    def _():
                        gather_copy(way, gathered.at[origin, block(c)], origin, c).start()

        c = i - (n - 1)

        @pl.when(c >= 0)
        def _():
            first_half(c)

        return carry

    lax.fori_loop(0, count + n - 1, gather_step, 0)

    def end_copy(slot, j):
        return pltpu.make_async_remote_copy(
            src_ref=state,
            dst_ref=ends.at[slot],
            send_sem=end_send.at[j],
            recv_sem=end_recv.at[slot],
            device_id={"context": j},
            device_id_type=MESH,
        )

    for j in range(1, contexts):
        @pl.when(k < j)
        def _():
            end_copy(k, j).start()

    for j in range(1, contexts):
        @pl.when(k < j)
        def _():
            end_copy(k, j).wait_send()

    state[...] = jnp.zeros_like(state)
    for j in range(contexts - 1):
        @pl.when(j < k)
        def _():
            end_copy(j, 0).wait_recv()
            state[...] = state[...] * decay_block[...] + ends[j]

    def second_half(c):
        factor = decay[...]
        weight = amp[...]

        def token_step(r, now):
            at = pl.ds(pl.multiple_of(c * piece + r * 8, 8), 8)
            u = drive[at]
            conv = []
            for t in range(8):
                now = now * factor + u[t : t + 1]
                conv.append(jnp.sum(now * weight, axis=0, keepdims=True))
            gated[pl.ds(pl.multiple_of(r * 8, 8), 8)] = query[at] * jnp.concatenate(conv, axis=0)
            return now

        state[...] = lax.fori_loop(0, piece // 8, token_step, state[...])
        rounded = gated[...].astype(jnp.bfloat16)
        for o in range(n):
            part[o, block(c)] = jnp.dot(
                rounded, wout[o], preferred_element_type=jnp.float32
            ).astype(jnp.bfloat16)

    def sum_copy(way, o, c):
        side = 0 if way > 0 else 1
        return pltpu.make_async_remote_copy(
            src_ref=part.at[o, block(c)],
            dst_ref=landed.at[side, o, block(c)],
            send_sem=rs_send.at[o, c],
            recv_sem=rs_recv.at[side, o, c],
            device_id={"tensor": z + way},
            device_id_type=MESH,
        )

    def sum_step(i, carry):
        @pl.when(i < count)
        def _():
            second_half(i)

        for way, c, first in ((1, i - z, z == 0), (-1, i - (n - 1 - z), z == n - 1)):
            side = 0 if way > 0 else 1
            for o in range(n) if way < 0 else range(n - 1, -1, -1):
                @pl.when((c >= 0) & (c < count) & ((o - z) * way > 0))
                def _():
                    @pl.when(jnp.logical_not(first))
                    def _():
                        sum_copy(way, o, c).wait_recv()
                        part[o, block(c)] = (
                            part[o, block(c)].astype(jnp.float32)
                            + landed[side, o, block(c)].astype(jnp.float32)
                        ).astype(jnp.bfloat16)

                    sum_copy(way, o, c).start()

        c = i - (n - 1)

        @pl.when(c >= 0)
        def _():
            @pl.when(z > 0)
            def _():
                sum_copy(1, z, c).wait_recv()

            @pl.when(z < n - 1)
            def _():
                sum_copy(-1, z, c).wait_recv()

            def own():
                return part[z, block(c)].astype(jnp.float32)

            def arrived(side):
                return landed[side, z, block(c)].astype(jnp.float32)

            @pl.when(z == 0)
            def _():
                out[block(c)] = (own() + arrived(1)).astype(out.dtype)

            @pl.when(z == n - 1)
            def _():
                out[block(c)] = (own() + arrived(0)).astype(out.dtype)

            @pl.when((z > 0) & (z < n - 1))
            def _():
                out[block(c)] = (own() + arrived(0) + arrived(1)).astype(out.dtype)

        return carry

    lax.fori_loop(0, count + n - 1, sum_step, 0)

    @pl.when(k < contexts - 1)
    def _():
        for zz in range(n):
            rim_copy(z, zz).wait_send()

    def drain(c, carry):
        for o in range(n):
            @pl.when((o <= z) & (z < n - 1))
            def _():
                gather_copy(1, gathered.at[o, block(c)], o, c).wait_send()

            @pl.when((o >= z) & (z > 0))
            def _():
                gather_copy(-1, gathered.at[o, block(c)], o, c).wait_send()

            @pl.when(o > z)
            def _():
                sum_copy(1, o, c).wait_send()

            @pl.when(o < z)
            def _():
                sum_copy(-1, o, c).wait_send()

        return carry

    lax.fori_loop(0, count, drain, 0)


def per_device(tokens, in_weight, short_filter, mode_weight, decay_rate, out_weight):
    n = lax.axis_size("tensor")
    contexts = lax.axis_size("context")
    rows, share = tokens.shape
    ch = in_weight.shape[2]
    modes = decay_rate.shape[1]
    count = 8 if rows % 128 == 0 else 1
    piece = rows // count
    win = in_weight.reshape(n, share, 3, ch).transpose(2, 0, 1, 3)
    wout = out_weight.reshape(ch, n, share).transpose(1, 0, 2)
    filt = short_filter.astype(jnp.float32).transpose(1, 0, 2)
    decay = jnp.exp(-decay_rate).T
    decay_block = jnp.exp(-decay_rate * rows).T
    amp = (mode_weight * jnp.sqrt(2.0 * decay_rate)).T
    vmem = pl.BlockSpec(memory_space=pltpu.VMEM)
    anywhere = pl.BlockSpec(memory_space=pl.ANY)
    flops = 2 * rows * n * share * ch * 4
    return pl.pallas_call(
        functools.partial(kernel, n, contexts, count),
        out_shape=jax.ShapeDtypeStruct((rows, share), jnp.bfloat16),
        in_specs=[anywhere] * 3 + [vmem] * 4,
        out_specs=vmem,
        scratch_shapes=[
            pltpu.VMEM((n, rows, share), jnp.bfloat16),
            pltpu.VMEM((n, RIM, share), jnp.bfloat16),
            pltpu.VMEM((3, n, share, ch), jnp.bfloat16),
            pltpu.VMEM((n, ch, share), jnp.bfloat16),
            pltpu.VMEM((3, HEAD + piece, ch), jnp.float32),
            pltpu.VMEM((rows, ch), jnp.float32),
            pltpu.VMEM((rows, ch), jnp.float32),
            pltpu.VMEM((piece, ch), jnp.float32),
            pltpu.VMEM((modes, ch), jnp.float32),
            pltpu.VMEM((contexts, modes, ch), jnp.float32),
            pltpu.VMEM((n, rows, share), jnp.bfloat16),
            pltpu.VMEM((2, n, rows, share), jnp.bfloat16),
            pltpu.SemaphoreType.DMA((3,)),
            pltpu.SemaphoreType.DMA((n,)),
            pltpu.SemaphoreType.DMA((n,)),
            pltpu.SemaphoreType.DMA((2, n, count)),
            pltpu.SemaphoreType.DMA((n, count)),
            pltpu.SemaphoreType.DMA((contexts,)),
            pltpu.SemaphoreType.DMA((contexts,)),
            pltpu.SemaphoreType.DMA((n, count)),
            pltpu.SemaphoreType.DMA((2, n, count)),
        ],
        compiler_params=pltpu.CompilerParams(
            collective_id=0, has_side_effects=True, vmem_limit_bytes=56 * 1024 * 1024
        ),
        cost_estimate=pl.CostEstimate(flops=flops, bytes_accessed=9_000_000, transcendentals=0),
    )(tokens, win, wout, filt, decay, amp, decay_block)


def solution(mesh):
    placed = (
        P(("groups", "context"), "tensor"),
        P(None, None, "tensor"),
        P(None, None, "tensor"),
        P("tensor", None),
        P("tensor", None),
        P("tensor", None),
    )
    return jax.shard_map(
        per_device,
        mesh=mesh,
        in_specs=placed,
        out_specs=P(("groups", "context"), "tensor"),
        check_vma=False,
    )
```

time: 420 us -> 180 us (0.43)
  matrix products: 184 us -> 0 us
  waiting for transfers between devices: 173 us -> 0 us
  Pallas kernels: 0 us -> 158 us
  other arithmetic: 21.6 us -> 2.8 us
  between operations: 13.5 us -> 0.02 us
    dot_general x9 -> x0, matrix products: 184 us -> none  [the longest x1 128 us: local_conv(): inside = jnp.einsum('tsc,bsc->btc', toeplitz, blocks, precision=HIGH)]
    pallas_call x0 -> x1, Pallas kernels: none -> 158 us  [per_device(): pl.pallas_call(functools.partial(kernel, n, contexts, count), out_shape=j...]
    all_gather x2 -> x0, waiting for transfers between devices: 98.4 us -> none  [the longest x1 79.7 us: per_device(): lax.all_gather(tokens, 'tensor', axis=1, tiled=True)]
    reduce_scatter x1 -> x0, waiting for transfers between devices: 72.8 us -> none  [per_device(): lax.psum_scatter(partial_sums.astype(jnp.bfloat16), 'tensor', scatter_dim...]
    add x5 -> x0, other arithmetic: 9.98 us -> none  [the longest x1 9.55 us: per_device(): filtered + short_filter[tap_number].astype(jnp.float32)[None] * padded[be...]
    while x8 -> x0, local copies, waits for them, and re-layouts: 8.8 us -> none
    convert_element_type x4 -> x0, other arithmetic: 8.24 us -> none  [the longest x1 6.16 us: per_device(): lax.all_gather(drive.astype(jnp.bfloat16), 'context', axis=0, tiled=True)]
    unnamed x31 -> x3, local copies, waits for them, and re-layouts: 8.14 us -> 13.4 us
  transfers between devices with their start and end apart: 4 -> 0, of which waited for: 4 -> 0; matrix products, arithmetic and copies ran while one was open for 4% -> 0% of each run, Pallas kernels for 0% -> 0%
where the time goes in v1:
time: 180 us; the launch traced here: 179 us
  Pallas kernels  158 us (88%)
  local copies, waits for them, and re-layouts  17.9 us (10%)
  other arithmetic  2.8 us (2%)
    pallas_call x1, Pallas kernels, per_device(): pl.pallas_call(functools.partial(kernel, n, contexts, count), out_shape=j...  158 us
    unnamed x3, local copies, waits for them, and re-layouts  13.4 us

profile of v1, /device:TPU:0, one launch (start us, length us, event | category | flops | bytes accessed | tf_op | source)
XLA Modules:
  0.0 179.1 jit_solution(10894927187143514297)
XLA Ops:
  0.0 1.4 convert_bitcast_fusion.filt
  1.4 1.4 exponential_bitcast_fusion
  2.8 2.3 %copy.13.tok = bf16[1024,480]{1,0:T(8,128)(2,1)} copy(bf16[1024,480]{0,1:T(8,128)(2,1)} %param.6) | data formatting | bytes 1966080 | tf_op args[0]
  5.1 2.6 %copy.11 = bf16[480,1920]{0,1:T(8,128)(2,1)S(1)} copy(bf16[480,1920]{1,0:T(8,128)(2,1)} %param.11) | data formatting | bytes 3686400 | tf_op args[5]
  7.8 2.3 %copy.12 = bf16[480,4,480]{2,0,1:T(8,128)(2,1)} copy(bf16[480,4,480]{0,2,1:T(8,128)(2,1)S(1)} %bitcast.13) | data formatting | bytes 3686400 | tf_op jit(solution)/shard_map/reshape | solution.py:319
  10.1 8.4 %copy.10 = bf16[1920,3,480]{2,0,1:T(8,128)(2,1)} copy(bf16[1920,3,480]{0,2,1:T(8,128)(2,1)} %param.7) | data formatting | bytes 11059200 | tf_op args[1]
  18.5 158.4 %shard_map.64 = bf16[1024,480]{1,0:T(8,128)(2,1)} custom-call(bf16[1024,480]{1,0:T(8,128)(2,1)} %copy.13.tok, bf16[3,4,480,480]{3,2,1,0:T(8,128)(2,1)} %bitcast.14, bf16[4,480,480]{2,1,0:T(8,128)(2,1)} %bitcast.15, f32[3,7,480]{2,1,0:T(8,128)} %convert_bitcast_fusion.filt, f32[16,480]{1,0:T(8,128)} %get-tuple-element.7.decay, ...), custom_call_target="tpu_custom_call" | custom-call | flops 7549747200 | bytes 9000000 | tf_op jit(solution)/shard_map/pallas_call | solution.py:327
  176.9 2.2 %copy.14 = bf16[1024,480]{0,1:T(8,128)(2,1)} copy(bf16[1024,480]{1,0:T(8,128)(2,1)} %shard_map.64) | data formatting | bytes 1966080 | tf_op jit(solution)/shard_map/pallas_call | solution.py:327

commit v2 on v1

--- a/solution.py
+++ b/solution.py
@@ -13,22 +13,46 @@
 MESH = pl.DeviceIdType.MESH
 
 
+def flip(array):
+    height, width = array.shape
+    tall, wide = -(-height // 128) * 128, -(-width // 128) * 128
+    if wide > width:
+        array = jnp.concatenate([array, jnp.zeros((height, wide - width), array.dtype)], 1)
+    if tall > height:
+        array = jnp.concatenate([array, jnp.zeros((tall - height, wide), array.dtype)], 0)
+    return array.T[:width, :height]
+
+
+def stacked(gathered, c, n):
+    share, piece = gathered.shape[2:]
+    if share % 16 == 0:
+        return gathered[c].reshape(n * share, piece)
+    pieces = [gathered[c, o].astype(jnp.float32) for o in range(n)]
+    return jnp.concatenate(pieces, 0).astype(jnp.bfloat16)
+
+
 def kernel(
-    n, contexts, count, tok, win_hbm, wout_hbm, filt, decay, amp, decay_block, out,
-    gathered, rim, win, wout, window, query, drive, gated, state, ends, part, landed,
-    local_sem, rim_send, rim_recv, ag_send, ag_recv, end_send, end_recv, rs_send, rs_recv,
+    n, contexts, count, tok, win_hbm, wout_hbm, filt_in, weight_in, rate, out,
+    gathered, tail, rim, win, wout, window, query, drive, gated, state, ends, part, landed,
+    filt, decay, amp, decay_block, local_sem, tok_sem, rim_send, rim_recv, ag_send, ag_recv, end_send, end_recv, rs_send, rs_recv,
 ):
-    rows, ch = tok.shape
+    share, rows = tok.shape
+    ch = win.shape[1]
     piece = rows // count
     z = lax.axis_index("tensor")
     k = lax.axis_index("context")
 
     loads = [
-        pltpu.make_async_copy(tok, gathered.at[z], local_sem.at[0]),
-        pltpu.make_async_copy(win_hbm, win, local_sem.at[1]),
-        pltpu.make_async_copy(wout_hbm, wout, local_sem.at[2]),
+        pltpu.make_async_copy(win_hbm, win, local_sem.at[0]),
+        pltpu.make_async_copy(wout_hbm, wout, local_sem.at[1]),
     ]
-    for load in loads:
+    own_loads = [
+        pltpu.make_async_copy(
+            tok.at[:, pl.ds(c * piece, piece)], gathered.at[c, z], tok_sem.at[c]
+        )
+        for c in range(count)
+    ]
+    for load in own_loads + loads:
         load.start()
 
     barrier = pltpu.get_barrier_semaphore()
@@ -58,7 +82,7 @@
         side = 0 if way > 0 else 1
         return pltpu.make_async_remote_copy(
             src_ref=src,
-            dst_ref=gathered.at[origin, block(c)],
+            dst_ref=gathered.at[c, origin],
             send_sem=ag_send.at[side, origin, c],
             recv_sem=ag_recv.at[origin, c],
             device_id={"tensor": z + way},
@@ -69,11 +93,11 @@
         for way, here in ((1, z < n - 1), (-1, z > 0)):
             @pl.when(here)
             def _():
-                gather_copy(way, tok.at[block(c)], z, c).start()
+                gather_copy(way, gathered.at[c, z], z, c).start()
 
     def rim_copy(slot, zz):
         return pltpu.make_async_remote_copy(
-            src_ref=tok.at[pl.ds(rows - RIM, RIM)],
+            src_ref=tail,
             dst_ref=rim.at[slot],
             send_sem=rim_send.at[zz],
             recv_sem=rim_recv.at[slot],
@@ -81,21 +105,28 @@
             device_id_type=MESH,
         )
 
+    for load in own_loads:
+        load.wait()
+    send_own(0)
+
     @pl.when(k < contexts - 1)
     def _():
+        tail[...] = flip(gathered[count - 1, z].astype(jnp.float32))[piece - RIM :].astype(tail.dtype)
         for zz in range(n):
             rim_copy(z, zz).start()
 
-    send_own(0)
+    for stream in range(3):
+        filt[stream, pl.ds(0, TAPS)] = filt_in[stream].astype(jnp.float32)
+    decay[...] = jnp.exp(-rate[...])
+    decay_block[...] = jnp.exp(-rate[...] * rows)
+    amp[...] = weight_in[...] * jnp.sqrt(2.0 * rate[...])
+    state[...] = jnp.zeros_like(state)
     for load in loads:
         load.wait()
-    state[...] = jnp.zeros_like(state)
-
-    def project(stream, load):
-        acc = jnp.dot(load(0), win[stream, 0], preferred_element_type=jnp.float32)
-        for o in range(1, n):
-            acc += jnp.dot(load(o), win[stream, o], preferred_element_type=jnp.float32)
-        return acc.astype(jnp.bfloat16).astype(jnp.float32)
+
+    def project(stream, columns):
+        acc = jnp.dot(win[stream], columns, preferred_element_type=jnp.float32)
+        return flip(acc.astype(jnp.bfloat16).astype(jnp.float32))
 
     def first_half(c):
         @pl.when((c == 0) & (k == 0))
@@ -107,11 +138,16 @@
         def _():
             for o in range(n):
                 rim_copy(o, 0).wait_recv()
+            zeros = jnp.zeros((piece - RIM, share), jnp.float32)
+            columns = jnp.concatenate(
+                [flip(jnp.concatenate([rim[o].astype(jnp.float32), zeros], 0)) for o in range(n)], 0
+            ).astype(jnp.bfloat16)
             for stream in range(3):
-                window[stream, pl.ds(0, HEAD)] = project(stream, lambda o: rim[o])[RIM - HEAD :]
-
+                window[stream, pl.ds(0, HEAD)] = project(stream, columns)[RIM - HEAD : RIM]
+
+        columns = stacked(gathered, c, n)
         for stream in range(3):
-            window[stream, pl.ds(HEAD, piece)] = project(stream, lambda o: gathered[o, block(c)])
+            window[stream, pl.ds(HEAD, piece)] = project(stream, columns)
 
         def filter_step(r, carry):
             streams = []
@@ -150,11 +186,11 @@
             for way, origin, more in ((1, z - d, z < n - 1), (-1, z + d, z > 0)):
                 @pl.when((c >= 0) & (c < count) & (origin >= 0) & (origin < n))
                 def _():
-                    gather_copy(way, gathered.at[origin, block(c)], origin, c).wait_recv()
+                    gather_copy(way, gathered.at[c, origin], origin, c).wait_recv()
 
                     @pl.when(more)
                     def _():
-                        gather_copy(way, gathered.at[origin, block(c)], origin, c).start()
+                        gather_copy(way, gathered.at[c, origin], origin, c).start()
 
         c = i - (n - 1)
 
@@ -209,16 +245,15 @@
 
         state[...] = lax.fori_loop(0, piece // 8, token_step, state[...])
         rounded = gated[...].astype(jnp.bfloat16)
+        mixed = flip(jnp.dot(rounded, wout[...], preferred_element_type=jnp.float32))
         for o in range(n):
-            part[o, block(c)] = jnp.dot(
-                rounded, wout[o], preferred_element_type=jnp.float32
-            ).astype(jnp.bfloat16)
+            part[c, o] = mixed[o * share : (o + 1) * share].astype(jnp.bfloat16)
 
     def sum_copy(way, o, c):
         side = 0 if way > 0 else 1
         return pltpu.make_async_remote_copy(
-            src_ref=part.at[o, block(c)],
-            dst_ref=landed.at[side, o, block(c)],
+            src_ref=part.at[c, o],
+            dst_ref=landed.at[side, c, o],
             send_sem=rs_send.at[o, c],
             recv_sem=rs_recv.at[side, o, c],
             device_id={"tensor": z + way},
@@ -238,9 +273,9 @@
                     @pl.when(jnp.logical_not(first))
                     def _():
                         sum_copy(way, o, c).wait_recv()
-                        part[o, block(c)] = (
-                            part[o, block(c)].astype(jnp.float32)
-                            + landed[side, o, block(c)].astype(jnp.float32)
+                        part[c, o] = (
+                            part[c, o].astype(jnp.float32)
+                            + landed[side, c, o].astype(jnp.float32)
                         ).astype(jnp.bfloat16)
 
                     sum_copy(way, o, c).start()
@@ -258,22 +293,22 @@
                 sum_copy(-1, z, c).wait_recv()
 
             def own():
-                return part[z, block(c)].astype(jnp.float32)
+                return part[c, z].astype(jnp.float32)
 
             def arrived(side):
-                return landed[side, z, block(c)].astype(jnp.float32)
+                return landed[side, c, z].astype(jnp.float32)
 
             @pl.when(z == 0)
             def _():
-                out[block(c)] = (own() + arrived(1)).astype(out.dtype)
+                out[:, block(c)] = (own() + arrived(1)).astype(out.dtype)
 
             @pl.when(z == n - 1)
             def _():
-                out[block(c)] = (own() + arrived(0)).astype(out.dtype)
+                out[:, block(c)] = (own() + arrived(0)).astype(out.dtype)
 
             @pl.when((z > 0) & (z < n - 1))
             def _():
-                out[block(c)] = (own() + arrived(0) + arrived(1)).astype(out.dtype)
+                out[:, block(c)] = (own() + arrived(0) + arrived(1)).astype(out.dtype)
 
         return carry
 
@@ -288,11 +323,11 @@
         for o in range(n):
             @pl.when((o <= z) & (z < n - 1))
             def _():
-                gather_copy(1, gathered.at[o, block(c)], o, c).wait_send()
+                gather_copy(1, gathered.at[c, o], o, c).wait_send()
 
             @pl.when((o >= z) & (z > 0))
             def _():
-                gather_copy(-1, gathered.at[o, block(c)], o, c).wait_send()
+                gather_copy(-1, gathered.at[c, o], o, c).wait_send()
 
             @pl.when(o > z)
             def _():
@@ -313,36 +348,36 @@
     rows, share = tokens.shape
     ch = in_weight.shape[2]
     modes = decay_rate.shape[1]
-    count = 8 if rows % 128 == 0 else 1
-    piece = rows // count
-    win = in_weight.reshape(n, share, 3, ch).transpose(2, 0, 1, 3)
-    wout = out_weight.reshape(ch, n, share).transpose(1, 0, 2)
-    filt = short_filter.astype(jnp.float32).transpose(1, 0, 2)
-    decay = jnp.exp(-decay_rate).T
-    decay_block = jnp.exp(-decay_rate * rows).T
-    amp = (mode_weight * jnp.sqrt(2.0 * decay_rate)).T
+    piece = 128
+    count = rows // piece
     vmem = pl.BlockSpec(memory_space=pltpu.VMEM)
     anywhere = pl.BlockSpec(memory_space=pl.ANY)
     flops = 2 * rows * n * share * ch * 4
-    return pl.pallas_call(
+    out = pl.pallas_call(
         functools.partial(kernel, n, contexts, count),
-        out_shape=jax.ShapeDtypeStruct((rows, share), jnp.bfloat16),
-        in_specs=[anywhere] * 3 + [vmem] * 4,
+        out_shape=jax.ShapeDtypeStruct((share, rows), jnp.bfloat16),
+        in_specs=[anywhere] * 3 + [vmem] * 3,
         out_specs=vmem,
         scratch_shapes=[
-            pltpu.VMEM((n, rows, share), jnp.bfloat16),
+            pltpu.VMEM((count, n, share, piece), jnp.bfloat16),
+            pltpu.VMEM((RIM, share), jnp.bfloat16),
             pltpu.VMEM((n, RIM, share), jnp.bfloat16),
-            pltpu.VMEM((3, n, share, ch), jnp.bfloat16),
-            pltpu.VMEM((n, ch, share), jnp.bfloat16),
+            pltpu.VMEM((3, ch, n * share), jnp.bfloat16),
+            pltpu.VMEM((ch, n * share), jnp.bfloat16),
             pltpu.VMEM((3, HEAD + piece, ch), jnp.float32),
             pltpu.VMEM((rows, ch), jnp.float32),
             pltpu.VMEM((rows, ch), jnp.float32),
             pltpu.VMEM((piece, ch), jnp.float32),
             pltpu.VMEM((modes, ch), jnp.float32),
             pltpu.VMEM((contexts, modes, ch), jnp.float32),
-            pltpu.VMEM((n, rows, share), jnp.bfloat16),
-            pltpu.VMEM((2, n, rows, share), jnp.bfloat16),
-            pltpu.SemaphoreType.DMA((3,)),
+            pltpu.VMEM((count, n, share, piece), jnp.bfloat16),
+            pltpu.VMEM((2, count, n, share, piece), jnp.bfloat16),
+            pltpu.VMEM((3, 8, ch), jnp.float32),
+            pltpu.VMEM((modes, ch), jnp.float32),
+            pltpu.VMEM((modes, ch), jnp.float32),
+            pltpu.VMEM((modes, ch), jnp.float32),
+            pltpu.SemaphoreType.DMA((2,)),
+            pltpu.SemaphoreType.DMA((count,)),
             pltpu.SemaphoreType.DMA((n,)),
             pltpu.SemaphoreType.DMA((n,)),
             pltpu.SemaphoreType.DMA((2, n, count)),
@@ -356,7 +391,15 @@
             collective_id=0, has_side_effects=True, vmem_limit_bytes=56 * 1024 * 1024
         ),
         cost_estimate=pl.CostEstimate(flops=flops, bytes_accessed=9_000_000, transcendentals=0),
-    )(tokens, win, wout, filt, decay, amp, decay_block)
+    )(
+        tokens.T,
+        in_weight.transpose(1, 2, 0),
+        out_weight,
+        short_filter.transpose(1, 0, 2),
+        mode_weight.T,
+        decay_rate.T,
+    )
+    return out.T
 
 
 def solution(mesh):

time: 180 us -> 155 us (0.86)
  local copies, waits for them, and re-layouts: 17.9 us -> 2.21 us
  Pallas kernels: 158 us -> 152 us
  other arithmetic: 2.8 us -> 0 us
    unnamed x3 -> x1, local copies, waits for them, and re-layouts: 13.4 us -> 2.21 us
    pallas_call x1, Pallas kernels: 158 us -> 152 us  [per_device(): pl.pallas_call(functools.partial(kernel, n, contexts, count), out_shape=j...]
    transpose x2 -> x0, other arithmetic: 2.8 us -> none  [the longest x1 1.43 us: per_device(): decay_block = jnp.exp(-decay_rate * rows).T]
    reshape x1 -> x0, local copies, waits for them, and re-layouts: 2.32 us -> none  [per_device(): wout = out_weight.reshape(ch, n, share).transpose(1, 0, 2)]
    pallas_call x1 -> x0, local copies, waits for them, and re-layouts: 2.25 us -> none  [per_device(): pl.pallas_call(functools.partial(kernel, n, contexts, count), out_shape=j...]
where the time goes in v2:
time: 155 us; the launch traced here: 154 us
  Pallas kernels  152 us (98%)
  local copies, waits for them, and re-layouts  2.21 us (1%)
    pallas_call x1, Pallas kernels, per_device(): pl.pallas_call(functools.partial(kernel, n, contexts, count), out_shape=j...  152 us

profile of v2, /device:TPU:0, one launch (start us, length us, event | category | flops | bytes accessed | tf_op | source)
XLA Modules:
  0.0 154.1 jit_solution(15406481387133398721)
XLA Ops:
  0.0 151.8 %shard_map.64 = bf16[480,1024]{1,0:T(8,128)(2,1)} custom-call(bf16[480,1024]{1,0:T(8,128)(2,1)} %bitcast.8, bf16[3,480,1920]{2,1,0:T(8,128)(2,1)} %bitcast.7, bf16[480,1920]{1,0:T(8,128)(2,1)} %wout_hbm.1, bf16[3,7,480]{2,1,0:T(8,128)(2,1)} %bitcast.11, f32[16,480]{1,0:T(8,128)} %bitcast.9, f32[16,480]{1,0:T(8,128)} %bitcast.10), custom_call_target="tpu_custom_call" | custom-call | flops 7549747200 | bytes 9000000 | tf_op jit(solution)/shard_map/pallas_call | solution.py:356
  151.9 2.2 %copy.8 = bf16[1024,480]{0,1:T(8,128)(2,1)} copy(bf16[1024,480]{0,1:T(8,128)(2,1)} %bitcast.6) | data formatting | bytes 1966080

commit v3 on v2

v3 whole, which is shorter than its diff:
```python
import functools

import jax
import jax.numpy as jnp
from jax import lax
from jax.experimental import pallas as pl
from jax.experimental.pallas import tpu as pltpu
from jax.sharding import PartitionSpec as P

TAPS = 7
HEAD = 8
MESH = pl.DeviceIdType.MESH


def flip(array):
    height, width = array.shape
    tall, wide = -(-height // 128) * 128, -(-width // 128) * 128
    if wide > width:
        array = jnp.concatenate([array, jnp.zeros((height, wide - width), array.dtype)], 1)
    if tall > height:
        array = jnp.concatenate([array, jnp.zeros((tall - height, wide), array.dtype)], 0)
    return array.T[:width, :height]


def stacked(gathered, c, n):
    share, piece = gathered.shape[2:]
    if share % 16 == 0:
        return gathered[c].reshape(n * share, piece)
    pieces = [gathered[c, o].astype(jnp.float32) for o in range(n)]
    return jnp.concatenate(pieces, 0).astype(jnp.bfloat16)


def kernel(
    n, contexts, count, tok, win_hbm, wout_hbm, filt_in, weight_in, rate, out,
    gathered, tails, rims, win, wout, window, query, drive, gated, state, begin, ends, part,
    landed, done, returned, filt, decay, amp, decay_piece,
    local_sem, own_sem, deal_send, deal_recv, rim_send, rim_recv, ag_send, ag_recv,
    end_send, end_recv, rs_send, rs_recv, out_send, out_recv,
):
    share, rows = tok.shape
    ch = win.shape[1]
    piece = rows // count
    z = lax.axis_index("tensor")
    k = lax.axis_index("context")

    loads = [
        pltpu.make_async_copy(win_hbm, win, local_sem.at[0]),
        pltpu.make_async_copy(wout_hbm, wout, local_sem.at[1]),
    ]
    for load in loads:
        load.start()

    barrier = pltpu.get_barrier_semaphore()

    def signal(here, context, tensor):
        @pl.when(here)
        def _():
            pl.semaphore_signal(
                barrier, inc=1, device_id={"context": context, "tensor": tensor}, device_id_type=MESH
            )

    peers = [(z > 0, k, z - 1), (z < n - 1, k, z + 1)]
    for j in range(contexts):
        peers.append((k != j, j, z))
    for here, context, tensor in peers:
        signal(here, context, tensor)
    total = functools.reduce(lambda x, y: x + y, [here.astype(jnp.int32) for here, _, _ in peers])
    pl.semaphore_wait(barrier, total)

    def block(c):
        return pl.ds(pl.multiple_of(c * piece, piece), piece)

    def dealt(c):
        g = k * count + c
        return g % contexts, g // contexts

    def owner(slab):
        g = slab * contexts + k
        return g // count, g % count

    def deal_copy(c, context, slab):
        return pltpu.make_async_remote_copy(
            src_ref=tok.at[:, block(c)],
            dst_ref=gathered.at[slab, z],
            send_sem=deal_send.at[c],
            recv_sem=deal_recv.at[slab],
            device_id={"context": context},
            device_id_type=MESH,
        )

    def own_copy(c, slab):
        return pltpu.make_async_copy(tok.at[:, block(c)], gathered.at[slab, z], own_sem.at[slab])

    for c in range(count):
        context, slab = dealt(c)

        @pl.when(context == k)
        def _():
            own_copy(c, slab).start()

        @pl.when(context != k)
        def _():
            deal_copy(c, context, slab).start()

    def gather_copy(way, origin, c):
        side = 0 if way > 0 else 1
        return pltpu.make_async_remote_copy(
            src_ref=gathered.at[c, origin],
            dst_ref=gathered.at[c, origin],
            send_sem=ag_send.at[side, origin, c],
            recv_sem=ag_recv.at[origin, c],
            device_id={"tensor": z + way},
            device_id_type=MESH,
        )

    def send_own(slab):
        context, c = owner(slab)

        @pl.when(context == k)
        def _():
            own_copy(c, slab).wait()

        @pl.when(context != k)
        def _():
            deal_copy(c, context, slab).wait_recv()

        for way, here in ((1, z < n - 1), (-1, z > 0)):
            @pl.when(here)
            def _():
                gather_copy(way, z, slab).start()

    send_own(0)
    for stream in range(3):
        filt[stream, pl.ds(0, TAPS)] = filt_in[stream].astype(jnp.float32)
    decay[...] = jnp.exp(-rate[...])
    decay_piece[...] = jnp.exp(-rate[...] * piece)
    amp[...] = weight_in[...] * jnp.sqrt(2.0 * rate[...])
    state[...] = jnp.zeros_like(state)
    for load in loads:
        load.wait()

    def rim_copy(c, slab, context):
        return pltpu.make_async_remote_copy(
            src_ref=tails.at[c],
            dst_ref=rims.at[slab],
            send_sem=rim_send.at[c],
            recv_sem=rim_recv.at[slab],
            device_id={"context": context},
            device_id_type=MESH,
        )

    def rim_target(c):
        wraps = (k == contexts - 1).astype(jnp.int32)
        return c + wraps, (k + 1) % contexts

    def project(c):
        columns = stacked(gathered, c, n)
        for stream in range(3):
            acc = jnp.dot(win[stream], columns, preferred_element_type=jnp.float32)
            window[stream, pl.ds(HEAD, piece)] = flip(acc.astype(jnp.bfloat16).astype(jnp.float32))
        for stream in range(3):
            tails[c, stream] = window[stream, pl.ds(piece, HEAD)]
        slab, context = rim_target(c)

        @pl.when(slab < count)
        def _():
            rim_copy(c, slab, context).start()

    def end_copy(c, slot, context):
        return pltpu.make_async_remote_copy(
            src_ref=ends.at[c, slot],
            dst_ref=ends.at[c, slot],
            send_sem=end_send.at[c, context],
            recv_sem=end_recv.at[c, slot],
            device_id={"context": context},
            device_id_type=MESH,
        )

    def first_half(c):
        starts = (c == 0) & (k == 0)

        @pl.when(starts)
        def _():
            for stream in range(3):
                window[stream, pl.ds(0, HEAD)] = jnp.zeros((HEAD, ch), jnp.float32)

        @pl.when(jnp.logical_not(starts))
        def _():
            rim_copy(0, c, 0).wait_recv()
            for stream in range(3):
                window[stream, pl.ds(0, HEAD)] = rims[c, stream]

        def filter_step(r, carry):
            streams = []
            for stream in range(3):
                seen = window[stream, pl.ds(pl.multiple_of(r * 16, 8), 16 + HEAD)]
                total = filt[stream, pl.ds(0, 1)] * seen[HEAD:]
                for tap in range(1, TAPS):
                    total += filt[stream, pl.ds(tap, 1)] * seen[HEAD - tap : HEAD - tap + 16]
                streams.append(total)
            at = pl.ds(pl.multiple_of(c * piece + r * 16, 16), 16)
            query[at] = streams[0]
            drive[at] = streams[1] * streams[2]
            return carry

        lax.fori_loop(0, piece // 16, filter_step, 0)
        factor = decay[...]

        def state_step(r, now):
            u = drive[pl.ds(pl.multiple_of(c * piece + r * 8, 8), 8)]
            for t in range(8):
                now = now * factor + u[t : t + 1]
            return now

        ends[c, k] = lax.fori_loop(0, piece // 8, state_step, jnp.zeros_like(factor))
        for j in range(contexts):
            @pl.when(k != j)
            def _():
                end_copy(c, k, j).start()

    def second_half(c):
        factor = decay[...]
        weight = amp[...]
        for j in range(contexts):
            @pl.when(k != j)
            def _():
                end_copy(c, j, 0).wait_recv()

            @pl.when(k == j)
            def _():
                begin[...] = state[...]

            state[...] = state[...] * decay_piece[...] + ends[c, j]

        def token_step(r, now):
            at = pl.ds(pl.multiple_of(c * piece + r * 8, 8), 8)
            u = drive[at]
            conv = []
            for t in range(8):
                now = now * factor + u[t : t + 1]
                conv.append(jnp.sum(now * weight, axis=0, keepdims=True))
            gated[pl.ds(pl.multiple_of(r * 8, 8), 8)] = query[at] * jnp.concatenate(conv, axis=0)
            return now

        lax.fori_loop(0, piece // 8, token_step, begin[...])
        rounded = gated[...].astype(jnp.bfloat16)
        mixed = flip(jnp.dot(rounded, wout[...], preferred_element_type=jnp.float32))
        for o in range(n):
            part[c, o] = mixed[o * share : (o + 1) * share].astype(jnp.bfloat16)

    def sum_copy(way, o, c):
        side = 0 if way > 0 else 1
        return pltpu.make_async_remote_copy(
            src_ref=part.at[c, o],
            dst_ref=landed.at[side, c, o],
            send_sem=rs_send.at[o, c],
            recv_sem=rs_recv.at[side, o, c],
            device_id={"tensor": z + way},
            device_id_type=MESH,
        )

    def out_copy(slab, context, c):
        return pltpu.make_async_remote_copy(
            src_ref=done.at[slab],
            dst_ref=returned.at[c],
            send_sem=out_send.at[slab],
            recv_sem=out_recv.at[c],
            device_id={"context": context},
            device_id_type=MESH,
        )

    def sums(i):
        for way, c, first in ((1, i - z, z == 0), (-1, i - (n - 1 - z), z == n - 1)):
            side = 0 if way > 0 else 1
            for o in range(n) if way < 0 else range(n - 1, -1, -1):
                @pl.when((c >= 0) & (c < count) & ((o - z) * way > 0))
                def _():
                    @pl.when(jnp.logical_not(first))
                    def _():
                        sum_copy(way, o, c).wait_recv()
                        part[c, o] = (
                            part[c, o].astype(jnp.float32)
                            + landed[side, c, o].astype(jnp.float32)
                        ).astype(jnp.bfloat16)

                    sum_copy(way, o, c).start()

        c = i - (n - 1)

        @pl.when((c >= 0) & (c < count))
        def _():
            @pl.when(z > 0)
            def _():
                sum_copy(1, z, c).wait_recv()

            @pl.when(z < n - 1)
            def _():
                sum_copy(-1, z, c).wait_recv()

            def own():
                return part[c, z].astype(jnp.float32)

            def arrived(side):
                return landed[side, c, z].astype(jnp.float32)

            @pl.when(z == 0)
            def _():
                done[c] = (own() + arrived(1)).astype(out.dtype)

            @pl.when(z == n - 1)
            def _():
                done[c] = (own() + arrived(0)).astype(out.dtype)

            @pl.when((z > 0) & (z < n - 1))
            def _():
                done[c] = (own() + arrived(0) + arrived(1)).astype(out.dtype)

            context, place = owner(c)

            @pl.when(context != k)
            def _():
                out_copy(c, context, place).start()

    def step(i, carry):
        @pl.when(i + 1 < count)
        def _():
            send_own(i + 1)

        for d in range(n - 1, 0, -1):
            c = i - d
            for way, origin, more in ((1, z - d, z < n - 1), (-1, z + d, z > 0)):
                @pl.when((c >= 0) & (c < count) & (origin >= 0) & (origin < n))
                def _():
                    gather_copy(way, origin, c).wait_recv()

                    @pl.when(more)
                    def _():
                        gather_copy(way, origin, c).start()

        ready = i - (n - 1)

        @pl.when((ready >= 0) & (ready < count))
        def _():
            project(ready)

        @pl.when((ready >= 1) & (ready <= count))
        def _():
            second_half(ready - 1)

        @pl.when(ready >= 1)
        def _():
            sums(ready - 1)

        @pl.when((ready >= 0) & (ready < count))
        def _():
            first_half(ready)

        return carry

    lax.fori_loop(0, count + 2 * n - 1, step, 0)

    for c in range(count):
        context, slab = dealt(c)

        @pl.when(context == k)
        def _():
            out[:, pl.ds(c * piece, piece)] = done[slab]

        @pl.when(context != k)
        def _():
            out_copy(slab, context, c).wait_recv()
            out[:, pl.ds(c * piece, piece)] = returned[c]

    def drain(c, carry):
        context, slab = dealt(c)

        @pl.when(context != k)
        def _():
            deal_copy(c, context, slab).wait_send()

        context, place = owner(c)

        @pl.when(context != k)
        def _():
            out_copy(c, context, place).wait_send()

        slab, context = rim_target(c)

        @pl.when(slab < count)
        def _():
            rim_copy(c, slab, context).wait_send()

        for j in range(contexts):
            @pl.when(k != j)
            def _():
                end_copy(c, k, j).wait_send()

        for o in range(n):
            @pl.when((o <= z) & (z < n - 1))
            def _():
                gather_copy(1, o, c).wait_send()

            @pl.when((o >= z) & (z > 0))
            def _():
                gather_copy(-1, o, c).wait_send()

            @pl.when(o > z)
            def _():
                sum_copy(1, o, c).wait_send()

            @pl.when(o < z)
            def _():
                sum_copy(-1, o, c).wait_send()

        return carry

    lax.fori_loop(0, count, drain, 0)


def per_device(tokens, in_weight, short_filter, mode_weight, decay_rate, out_weight):
    n = lax.axis_size("tensor")
    contexts = lax.axis_size("context")
    rows, share = tokens.shape
    ch = in_weight.shape[2]
    modes = decay_rate.shape[1]
    piece = 128
    count = rows // piece
    vmem = pl.BlockSpec(memory_space=pltpu.VMEM)
    anywhere = pl.BlockSpec(memory_space=pl.ANY)
    flops = 2 * rows * n * share * ch * 4
    out = pl.pallas_call(
        functools.partial(kernel, n, contexts, count),
        out_shape=jax.ShapeDtypeStruct((share, rows), jnp.bfloat16),
        in_specs=[anywhere] * 3 + [vmem] * 3,
        out_specs=vmem,
        scratch_shapes=[
            pltpu.VMEM((count, n, share, piece), jnp.bfloat16),
            pltpu.VMEM((count, 3, HEAD, ch), jnp.float32),
            pltpu.VMEM((count, 3, HEAD, ch), jnp.float32),
            pltpu.VMEM((3, ch, n * share), jnp.bfloat16),
            pltpu.VMEM((ch, n * share), jnp.bfloat16),
            pltpu.VMEM((3, HEAD + piece, ch), jnp.float32),
            pltpu.VMEM((rows, ch), jnp.float32),
            pltpu.VMEM((rows, ch), jnp.float32),
            pltpu.VMEM((piece, ch), jnp.float32),
            pltpu.VMEM((modes, ch), jnp.float32),
            pltpu.VMEM((modes, ch), jnp.float32),
            pltpu.VMEM((count, contexts, modes, ch), jnp.float32),
            pltpu.VMEM((count, n, share, piece), jnp.bfloat16),
            pltpu.VMEM((2, count, n, share, piece), jnp.bfloat16),
            pltpu.VMEM((count, share, piece), jnp.bfloat16),
            pltpu.VMEM((count, share, piece), jnp.bfloat16),
            pltpu.VMEM((3, 8, ch), jnp.float32),
            pltpu.VMEM((modes, ch), jnp.float32),
            pltpu.VMEM((modes, ch), jnp.float32),
            pltpu.VMEM((modes, ch), jnp.float32),
            pltpu.SemaphoreType.DMA((2,)),
            pltpu.SemaphoreType.DMA((count,)),
            pltpu.SemaphoreType.DMA((count,)),
            pltpu.SemaphoreType.DMA((count,)),
            pltpu.SemaphoreType.DMA((count,)),
            pltpu.SemaphoreType.DMA((count,)),
            pltpu.SemaphoreType.DMA((2, n, count)),
            pltpu.SemaphoreType.DMA((n, count)),
            pltpu.SemaphoreType.DMA((count, contexts)),
            pltpu.SemaphoreType.DMA((count, contexts)),
            pltpu.SemaphoreType.DMA((n, count)),
            pltpu.SemaphoreType.DMA((2, n, count)),
            pltpu.SemaphoreType.DMA((count,)),
            pltpu.SemaphoreType.DMA((count,)),
        ],
        compiler_params=pltpu.CompilerParams(
            collective_id=0, has_side_effects=True, vmem_limit_bytes=56 * 1024 * 1024
        ),
        cost_estimate=pl.CostEstimate(flops=flops, bytes_accessed=9_000_000, transcendentals=0),
    )(
        tokens.T,
        in_weight.transpose(1, 2, 0),
        out_weight,
        short_filter.transpose(1, 0, 2),
        mode_weight.T,
        decay_rate.T,
    )
    return out.T


def solution(mesh):
    placed = (
        P(("groups", "context"), "tensor"),
        P(None, None, "tensor"),
        P(None, None, "tensor"),
        P("tensor", None),
        P("tensor", None),
        P("tensor", None),
    )
    return jax.shard_map(
        per_device,
        mesh=mesh,
        in_specs=placed,
        out_specs=P(("groups", "context"), "tensor"),
        check_vma=False,
    )
```

time: 155 us -> 128 us (0.83)
  Pallas kernels: 152 us -> 125 us
    pallas_call x1, Pallas kernels: 152 us -> 125 us  [per_device(): pl.pallas_call(functools.partial(kernel, n, contexts, count), out_shape=j...]
where the time goes in v3:
time: 128 us
  Pallas kernels  125 us (98%)
  local copies, waits for them, and re-layouts  2.21 us (2%)
    pallas_call x1, Pallas kernels, per_device(): pl.pallas_call(functools.partial(kernel, n, contexts, count), out_shape=j...  125 us

profile of v3, /device:TPU:0, one launch (start us, length us, event | category | flops | bytes accessed | tf_op | source)
XLA Modules:
  0.0 127.5 jit_solution(15520357293441398888)
XLA Ops:
  0.0 125.3 %shard_map.64 = bf16[480,1024]{1,0:T(8,128)(2,1)} custom-call(bf16[480,1024]{1,0:T(8,128)(2,1)} %bitcast.8, bf16[3,480,1920]{2,1,0:T(8,128)(2,1)} %bitcast.7, bf16[480,1920]{1,0:T(8,128)(2,1)} %wout_hbm.1, bf16[3,7,480]{2,1,0:T(8,128)(2,1)} %bitcast.11, f32[16,480]{1,0:T(8,128)} %bitcast.9, f32[16,480]{1,0:T(8,128)} %bitcast.10), custom_call_target="tpu_custom_call" | custom-call | flops 7549747200 | bytes 9000000 | tf_op jit(solution)/shard_map/pallas_call | solution.py:431
  125.3 2.2 %copy.8 = bf16[1024,480]{0,1:T(8,128)(2,1)} copy(bf16[1024,480]{0,1:T(8,128)(2,1)} %bitcast.6) | data formatting | bytes 1966080

commit v4 on v3

--- a/solution.py
+++ b/solution.py
@@ -32,7 +32,7 @@
 
 def kernel(
     n, contexts, count, tok, win_hbm, wout_hbm, filt_in, weight_in, rate, out,
-    gathered, tails, rims, win, wout, window, query, drive, gated, state, begin, ends, part,
+    gathered, tails, rims, win, wout, window, query, drive, local, carry_table, gated, state, begin, ends, part,
     landed, done, returned, filt, decay, amp, decay_piece,
     local_sem, own_sem, deal_send, deal_recv, rim_send, rim_recv, ag_send, ag_recv,
     end_send, end_recv, rs_send, rs_recv, out_send, out_recv,
@@ -129,15 +129,18 @@
             def _():
                 gather_copy(way, z, slab).start()
 
-    send_own(0)
-    for stream in range(3):
-        filt[stream, pl.ds(0, TAPS)] = filt_in[stream].astype(jnp.float32)
-    decay[...] = jnp.exp(-rate[...])
-    decay_piece[...] = jnp.exp(-rate[...] * piece)
-    amp[...] = weight_in[...] * jnp.sqrt(2.0 * rate[...])
-    state[...] = jnp.zeros_like(state)
-    for load in loads:
-        load.wait()
+    def prepare():
+        for stream in range(3):
+            filt[stream, pl.ds(0, TAPS)] = filt_in[stream].astype(jnp.float32)
+        decay[...] = jnp.exp(-rate[...])
+        decay_piece[...] = jnp.exp(-rate[...] * piece)
+        amp[...] = weight_in[...] * jnp.sqrt(2.0 * rate[...])
+        state[...] = jnp.zeros_like(state)
+        after = (lax.broadcasted_iota(jnp.int32, (piece, ch), 0) + 1).astype(jnp.float32)
+        for m in range(rate.shape[0]):
+            carry_table[m] = amp[pl.ds(m, 1)] * jnp.exp(-rate[pl.ds(m, 1)] * after)
+        for load in loads:
+            load.wait()
 
     def rim_copy(c, slab, context):
         return pltpu.make_async_remote_copy(
@@ -157,7 +160,7 @@
         columns = stacked(gathered, c, n)
         for stream in range(3):
             acc = jnp.dot(win[stream], columns, preferred_element_type=jnp.float32)
-            window[stream, pl.ds(HEAD, piece)] = flip(acc.astype(jnp.bfloat16).astype(jnp.float32))
+            window[stream, pl.ds(HEAD, piece)] = flip(acc.astype(jnp.bfloat16)).astype(jnp.float32)
         for stream in range(3):
             tails[c, stream] = window[stream, pl.ds(piece, HEAD)]
         slab, context = rim_target(c)
@@ -198,7 +201,7 @@
                 for tap in range(1, TAPS):
                     total += filt[stream, pl.ds(tap, 1)] * seen[HEAD - tap : HEAD - tap + 16]
                 streams.append(total)
-            at = pl.ds(pl.multiple_of(c * piece + r * 16, 16), 16)
+            at = pl.ds(pl.multiple_of(r * 16, 16), 16)
             query[at] = streams[0]
             drive[at] = streams[1] * streams[2]
             return carry
@@ -206,45 +209,47 @@
         lax.fori_loop(0, piece // 16, filter_step, 0)
         factor = decay[...]
 
-        def state_step(r, now):
-            u = drive[pl.ds(pl.multiple_of(c * piece + r * 8, 8), 8)]
-            for t in range(8):
-                now = now * factor + u[t : t + 1]
-            return now
-
-        ends[c, k] = lax.fori_loop(0, piece // 8, state_step, jnp.zeros_like(factor))
-        for j in range(contexts):
-            @pl.when(k != j)
-            def _():
-                end_copy(c, k, j).start()
-
-    def second_half(c):
-        factor = decay[...]
         weight = amp[...]
-        for j in range(contexts):
-            @pl.when(k != j)
-            def _():
-                end_copy(c, j, 0).wait_recv()
-
-            @pl.when(k == j)
-            def _():
-                begin[...] = state[...]
-
-            state[...] = state[...] * decay_piece[...] + ends[c, j]
 
         def token_step(r, now):
-            at = pl.ds(pl.multiple_of(c * piece + r * 8, 8), 8)
+            at = pl.ds(pl.multiple_of(r * 8, 8), 8)
             u = drive[at]
             conv = []
             for t in range(8):
                 now = now * factor + u[t : t + 1]
                 conv.append(jnp.sum(now * weight, axis=0, keepdims=True))
-            gated[pl.ds(pl.multiple_of(r * 8, 8), 8)] = query[at] * jnp.concatenate(conv, axis=0)
+            local[at] = jnp.concatenate(conv, axis=0)
             return now
 
-        lax.fori_loop(0, piece // 8, token_step, begin[...])
-        rounded = gated[...].astype(jnp.bfloat16)
-        mixed = flip(jnp.dot(rounded, wout[...], preferred_element_type=jnp.float32))
+        ends[c, k] = lax.fori_loop(0, piece // 8, token_step, jnp.zeros_like(factor))
+        for j in range(contexts):
+            @pl.when(k != j)
+            def _():
+                end_copy(c, k, j).start()
+
+    def second_half(c):
+        for j in range(contexts):
+            @pl.when(k != j)
+            def _():
+                end_copy(c, j, 0).wait_recv()
+
+            @pl.when(k == j)
+            def _():
+                begin[...] = state[...]
+
+            state[...] = state[...] * decay_piece[...] + ends[c, j]
+
+        def carry_step(r, carry):
+            at = pl.ds(pl.multiple_of(r * 32, 32), 32)
+            conv = local[at]
+            for m in range(begin.shape[0]):
+                conv += carry_table[m, at] * begin[pl.ds(m, 1)]
+            gated[at] = (query[at] * conv).astype(jnp.bfloat16)
+            return carry
+
+        lax.fori_loop(0, piece // 32, carry_step, 0)
+        mixed = jnp.dot(gated[...], wout[...], preferred_element_type=jnp.float32)
+        mixed = flip(mixed.astype(jnp.bfloat16) if share % 16 == 0 else mixed)
         for o in range(n):
             part[c, o] = mixed[o * share : (o + 1) * share].astype(jnp.bfloat16)
 
@@ -322,10 +327,6 @@
                 out_copy(c, context, place).start()
 
     def step(i, carry):
-        @pl.when(i + 1 < count)
-        def _():
-            send_own(i + 1)
-
         for d in range(n - 1, 0, -1):
             c = i - d
             for way, origin, more in ((1, z - d, z < n - 1), (-1, z + d, z > 0)):
@@ -337,7 +338,15 @@
                     def _():
                         gather_copy(way, origin, c).start()
 
+        @pl.when(i < count)
+        def _():
+            send_own(i)
+
         ready = i - (n - 1)
+
+        @pl.when(i == 0)
+        def _():
+            prepare()
 
         @pl.when((ready >= 0) & (ready < count))
         def _():
@@ -440,9 +449,11 @@
             pltpu.VMEM((3, ch, n * share), jnp.bfloat16),
             pltpu.VMEM((ch, n * share), jnp.bfloat16),
             pltpu.VMEM((3, HEAD + piece, ch), jnp.float32),
-            pltpu.VMEM((rows, ch), jnp.float32),
-            pltpu.VMEM((rows, ch), jnp.float32),
             pltpu.VMEM((piece, ch), jnp.float32),
+            pltpu.VMEM((piece, ch), jnp.float32),
+            pltpu.VMEM((piece, ch), jnp.float32),
+            pltpu.VMEM((modes, piece, ch), jnp.float32),
+            pltpu.VMEM((piece, ch), jnp.bfloat16),
             pltpu.VMEM((modes, ch), jnp.float32),
             pltpu.VMEM((modes, ch), jnp.float32),
             pltpu.VMEM((count, contexts, modes, ch), jnp.float32),

time: 128 us -> 125 us (0.977)
  Pallas kernels: 125 us -> 122 us
    pallas_call x1, Pallas kernels: 125 us -> 122 us  [per_device(): pl.pallas_call(functools.partial(kernel, n, contexts, count), out_shape=j...]
where the time goes in v4:
time: 125 us; the launch traced here: 124 us
  Pallas kernels  122 us (98%)
  local copies, waits for them, and re-layouts  2.21 us (2%)
    pallas_call x1, Pallas kernels, per_device(): pl.pallas_call(functools.partial(kernel, n, contexts, count), out_shape=j...  122 us

profile of v4, /device:TPU:0, one launch (start us, length us, event | category | flops | bytes accessed | tf_op | source)
XLA Modules:
  0.0 124.5 jit_solution(6352928362866604421)
XLA Ops:
  0.0 122.3 %shard_map.64 = bf16[480,1024]{1,0:T(8,128)(2,1)} custom-call(bf16[480,1024]{1,0:T(8,128)(2,1)} %bitcast.8, bf16[3,480,1920]{2,1,0:T(8,128)(2,1)} %bitcast.7, bf16[480,1920]{1,0:T(8,128)(2,1)} %wout_hbm.1, bf16[3,7,480]{2,1,0:T(8,128)(2,1)} %bitcast.11, f32[16,480]{1,0:T(8,128)} %bitcast.9, f32[16,480]{1,0:T(8,128)} %bitcast.10), custom_call_target="tpu_custom_call" | custom-call | flops 7549747200 | bytes 9000000 | tf_op jit(solution)/shard_map/pallas_call | solution.py:440
  122.3 2.2 %copy.8 = bf16[1024,480]{0,1:T(8,128)(2,1)} copy(bf16[1024,480]{0,1:T(8,128)(2,1)} %bitcast.6) | data formatting | bytes 1966080

commit v5 on v4

--- a/solution.py
+++ b/solution.py
@@ -338,9 +338,13 @@
                     def _():
                         gather_copy(way, origin, c).start()
 
-        @pl.when(i < count)
+        @pl.when(i <= 1)
         def _():
             send_own(i)
+
+        @pl.when((i >= 1) & (i + 1 < count))
+        def _():
+            send_own(i + 1)
 
         ready = i - (n - 1)
 

time: 125 us -> 123 us (0.984)
  Pallas kernels: 122 us -> 120 us
    pallas_call x1, Pallas kernels: 122 us -> 120 us  [per_device(): pl.pallas_call(functools.partial(kernel, n, contexts, count), out_shape=j...]
where the time goes in v5:
time: 123 us; the launch traced here: 122 us
  Pallas kernels  120 us (98%)
  local copies, waits for them, and re-layouts  2.21 us (2%)
    pallas_call x1, Pallas kernels, per_device(): pl.pallas_call(functools.partial(kernel, n, contexts, count), out_shape=j...  120 us

profile of v5, /device:TPU:0, one launch (start us, length us, event | category | flops | bytes accessed | tf_op | source)
XLA Modules:
  0.0 122.2 jit_solution(4015285093849314457)
XLA Ops:
  0.0 120.0 %shard_map.64 = bf16[480,1024]{1,0:T(8,128)(2,1)} custom-call(bf16[480,1024]{1,0:T(8,128)(2,1)} %bitcast.8, bf16[3,480,1920]{2,1,0:T(8,128)(2,1)} %bitcast.7, bf16[480,1920]{1,0:T(8,128)(2,1)} %wout_hbm.1, bf16[3,7,480]{2,1,0:T(8,128)(2,1)} %bitcast.11, f32[16,480]{1,0:T(8,128)} %bitcast.9, f32[16,480]{1,0:T(8,128)} %bitcast.10), custom_call_target="tpu_custom_call" | custom-call | flops 7549747200 | bytes 9000000 | tf_op jit(solution)/shard_map/pallas_call | solution.py:444
  120.0 2.2 %copy.8 = bf16[1024,480]{0,1:T(8,128)(2,1)} copy(bf16[1024,480]{0,1:T(8,128)(2,1)} %bitcast.6) | data formatting | bytes 1966080
